TPU v7x, 32 devices: a whole 2x2x4 slice. The times are simulated.
32 devices in a mesh: context: 8 (over y, x, core), tensor: 4 (over z).
Axes of the slice: x: 2, y: 2, z: 4, core: 2. Of those that a mesh axis runs over, the one named last changes fastest.
Arguments:
- projected: bfloat16 [3, 3072, 8192], P(None, 'context', 'tensor'), may hold values from -6 to 6
- taps: float32 [3, 3, 8192], P(None, None, 'tensor'), may hold values from -4 to 4
- filters: bfloat16 [512, 128], P('tensor'), may hold values from -0.5 to 0.5
- skip: float32 [8192], P('tensor'), may hold values from -4 to 4
- out_weight: bfloat16 [8192, 8192], P('tensor', 'context'), may hold values from -0.09375 to 0.09375
- positions: int32 [32], replicated, may hold values from 0 to 3071
Outputs:
- mixed: bfloat16 [3072, 8192], P('context', 'tensor')
- variant_states: bfloat16 [32, 8192], P('context', 'tensor')
All inputs are finite; a program needn't handle non-finite values.
Results may differ from a plain program's by a relative error of at most 0.018.
Values may be sent and summed in bfloat16 or wider, within the bound.
A program may use at most 192 MiB of HBM per device.

v0:
```python
import jax
import jax.numpy as jnp
from jax import lax
from jax.sharding import PartitionSpec as P

FLT = 128
GROUP = 16
SHORT = 3


def shifted(array, axis, by):
    size = lax.axis_size(axis)
    pairs = [(i, i + by) for i in range(size) if 0 <= i + by < size]
    return lax.ppermute(array, axis, pairs)


def short_filter(extended, weights, count):
    lags = SHORT - 1
    total = jnp.zeros((extended.shape[0], count, extended.shape[2]), jnp.float32)
    for lag in range(SHORT):
        total = total + weights[:, lag, None, :] * extended[
            :, lags - lag : lags - lag + count, :
        ].astype(jnp.float32)
    return total


def banded_filters(filters, rows):
    local_groups = filters.shape[0]
    span = FLT - 1 + rows
    reversed_taps = jnp.flip(filters, axis=1)
    padded_taps = jnp.concatenate(
        [reversed_taps, jnp.zeros((local_groups, rows), filters.dtype)], axis=1
    )
    tiled = jnp.tile(padded_taps, (1, rows))
    return tiled[:, : rows * span].reshape(local_groups, rows, span)


def on_device(projected, taps, filters, skip, out_weight, positions):
    rows = projected.shape[1]
    width = projected.shape[2]
    lags = SHORT - 1
    reach = FLT - 1
    rim = shifted(projected[:, rows - lags :, :], "context", 1)
    feat = short_filter(jnp.concatenate([rim, projected], axis=1), taps, rows)
    query = feat[0]
    product = (feat[1] * feat[2]).astype(jnp.bfloat16)
    prior = shifted(product[rows - reach :], "context", 1)
    extended = jnp.concatenate([prior, product], axis=0)
    span = reach + rows
    toeplitz = banded_filters(filters, rows)
    local_groups = filters.shape[0]
    conv = jnp.einsum(
        "gim,mgc->igc",
        toeplitz,
        extended.reshape(span, local_groups, GROUP),
        preferred_element_type=jnp.float32,
    ).reshape(rows, width)
    conv = conv + skip[None, :] * product.astype(jnp.float32)
    gated = (query * conv).astype(jnp.bfloat16)
    terms = jnp.dot(
        gated,
        lax.all_gather(out_weight, "context", axis=1, tiled=True),
        preferred_element_type=jnp.float32,
    )
    mixed = lax.psum_scatter(terms.astype(jnp.bfloat16), "tensor", scatter_dimension=1, tiled=True)
    offset = lax.axis_index("context") * rows
    local_sites = positions - offset
    one_hot = (local_sites[:, None] == jnp.arange(rows, dtype=jnp.int32)[None, :]).astype(
        jnp.bfloat16
    )
    picked_terms = jnp.dot(one_hot, mixed, preferred_element_type=jnp.float32)
    variant_states = lax.psum_scatter(
        picked_terms.astype(jnp.bfloat16), "context", scatter_dimension=0, tiled=True
    )
    return (mixed, variant_states)


def solution(mesh):
    return jax.shard_map(
        on_device,
        mesh=mesh,
        in_specs=(
            P(None, "context", "tensor"),
            P(None, None, "tensor"),
            P("tensor", None),
            P("tensor"),
            P("tensor", "context"),
            P(),
        ),
        out_specs=(P("context", "tensor"), P("context", "tensor")),
        check_vma=False,
    )
```

profile of v0, /device:TPU:0, one launch (start us, length us, event | category | flops | bytes accessed | tf_op | source)
XLA Modules:
  0.0 469.0 jit_solution(5184999887100844345)
XLA Ops:
  7.2 0.0 all-gather.2.cloned.1.call-start
  7.2 0.7 all-gather.2.cloned.1.call-update
  7.9 0.0 reduce-scatter.2.cloned.1.call-start
  7.9 0.9 slice.38
  8.9 2.4 collective-permute-start
  11.2 1.1 fusion.8
  12.4 0.8 rev.4
  13.3 19.8 %tile.4 = bf16[128,384,512]{2,1,0:T(8,128)(2,1)} broadcast(bf16[128,512]{1,0:T(8,128)(2,1)S(1)} %concatenate.11), dimensions={0,2} | broadcast | bytes 50462720 | tf_op jit(solution)/shard_map/tile | solution.py:34
  33.1 45.5 %copy.17 = bf16[16,8,384,512]{3,1,2,0:T(8,128)(2,1)} copy(bf16[16,8,384,512]{3,2,1,0:T(8,128)(2,1)} %bitcast.33) | data formatting | bytes 100663296
  78.6 36.1 %slice.54 = bf16[128,196224]{1,0:T(8,128)(2,1)} slice(bf16[128,196608]{1,0:T(8,128)(2,1)} %bitcast.34), slice={[0:128], [0:196224]} | slice | bytes 100466688 | tf_op jit(solution)/shard_map/slice | solution.py:35
  114.7 106.3 %reshape.23 = bf16[128,384,511]{2,1,0:T(8,128)(2,1)} reshape(bf16[128,196224]{1,0:T(8,128)(2,1)} %slice.54) | data formatting | bytes 100466688 | tf_op jit(solution)/shard_map/reshape | solution.py:35
  221.0 0.0 collective-permute-done
  221.0 9.3 %multiply_add_fusion = f32[3,384,2048]{2,1,0:T(8,128)S(1)} fusion(bf16[3,384,2048]{2,1,0:T(8,128)(2,1)} %param.6, bf16[3,2,2048]{2,1,0:T(2,128)(2,1)S(1)} %collective-permute-done, f32[3,2048]{1,0:T(4,128)S(1)} %get-tuple-element.5, f32[3,2048]{1,0:T(4,128)S(1)} %get-tuple-element.6, f32[3,2048]{1,0:T(4,128)S(1)} %bitcast.37), kind=kLoop, calls=%fused_computation.1 | loop fusion | flops 33030144 | bytes 14254080 | tf_op jit(solution)/shard_map/add | solution.py:21
  230.3 0.0 copy-start
  230.3 0.4 fusion.1
  230.8 0.0 copy-start.1
  230.8 0.1 slice_bitcast_fusion.1
  230.9 1.3 copy-done.1
  232.2 4.3 collective-permute-start.1
  236.5 0.4 fusion.14
  236.9 0.0 copy-done
  236.9 0.9 collective-permute-done.1
  237.8 0.4 pad_maximum_fusion.1
  238.2 2.6 copy.12
  240.8 20.4 %fusion.9 = f32[128,16,384]{2,1,0:T(8,128)S(1)} fusion(bf16[511,128,16]{0,2,1:T(8,128)(2,1)} %bitcast.36, bf16[128,384,511]{2,1,0:T(8,128)(2,1)} %reshape.23), kind=kOutput, calls=%fused_computation.24 | convolution fusion | flops 803733504 | bytes 55472128 | tf_op jit(solution)/shard_map/gim,mgc->igc/dot_general | solution.py:52
  261.2 0.0 copy-start.2
  261.2 2.4 copy.13
  263.6 0.0 all-gather.2.cloned.1.call-done
  263.6 0.0 copy-done.2
  263.6 23.0 %convolution_convert_fusion = bf16[384,8192]{1,0:T(8,128)(2,1)} fusion(bf16[2048,8192]{1,0:T(8,128)(2,1)} %all-gather.2.cloned.1.call-done, f32[3,384,2048]{2,1,0:T(8,128)} %copy-done, f32[384,2048]{1,0:T(8,128)} %copy.13, f32[2048]{0:T(1024)S(1)} %copy-done.2, bf16[1,384,2048]{2,1,0:T(8,128)(2,1)} %copy-done.1), kind=kOutput, calls=%fused_computation | convolution fusion | flops 12891979776 | bytes 47718400 | tf_op jit(solution)/shard_map/dot_general | solution.py:60
  286.6 0.0 copy-start.3
  286.6 0.0 copy-start.4
  286.6 0.0 reduce-scatter.2.cloned.1.call-update
  286.6 0.0 all-reduce.4.cloned.1.call-start
  286.7 0.6 copy-done.3
  287.3 117.3 %reduce-scatter.2.cloned.1.call-done = bf16[384,2048]{1,0:T(8,128)(2,1)} async-done(((bf16[384,8192]{1,0:T(8,128)(2,1)}), bf16[384,2048]{1,0:T(8,128)(2,1)}) %reduce-scatter.2.cloned.1.call-update) | async-done | bytes 1572880 | tf_op jit(solution)/shard_map/reduce_scatter | solution.py:65
  404.5 2.5 convolution_convert_fusion.1
  407.0 0.0 all-reduce.4.cloned.1.call-update
  407.0 0.0 copy-done.4
  407.0 0.6 dynamic-slice
  408.3 52.8 %all-reduce.4.cloned.1.call-done = bf16[32,2048]{1,0:T(8,128)(2,1)} async-done(((bf16[32,2048]{1,0:T(8,128)(2,1)}), bf16[32,2048]{1,0:T(8,128)(2,1)}) %all-reduce.4.cloned.1.call-update) | async-done | bytes 131088
  461.1 1.4 constant_dynamic-slice_fusion
  (4 shorter events, 0.1 us)
Async XLA Ops:
  7.2 256.4 %all-gather.2.cloned.1.call-start = ((), (), s32[]{:S(2)}) async-start(), calls=%async_computation.1 | async-start | bytes 37748736 | tf_op jit(solution)/shard_map/all_gather | solution.py:62
  7.9 396.6 %reduce-scatter.2.cloned.1.call-start = ((), (), s32[]{:S(2)}) async-start(), calls=%async_computation.2 | async-start | bytes 7864320 | tf_op jit(solution)/shard_map/reduce_scatter | solution.py:65
  8.9 212.1 %collective-permute-start = (bf16[3,2,2048]{2,1,0:T(2,128)(2,1)S(1)}, bf16[3,2,2048]{2,1,0:T(2,128)(2,1)S(1)}, u32[]{:S(2)}, u32[]{:S(2)}) collective-permute-start(bf16[3,2,2048]{2,1,0:T(2,128)(2,1)S(1)} %slice.38), channel_id=1, source_target_pairs={{0,4},{4,8},{8,12},{12,16},{16,20},{20,24},{24,28},{1,5},{5,9},{9,... | collective-permute-start | bytes 73736 | tf_op jit(solution)/shard_map/ppermute | solution.py:14
  230.3 6.6 %copy-start = (f32[3,384,2048]{2,1,0:T(8,128)}, f32[3,384,2048]{2,1,0:T(8,128)S(1)}, u32[]{:S(2)}) copy-start(f32[3,384,2048]{2,1,0:T(8,128)S(1)} %multiply_add_fusion) | copy-start | bytes 28311556
  230.8 1.4 copy-start.1
  232.2 5.6 %collective-permute-start.1 = (bf16[127,2048]{1,0:T(8,128)(2,1)S(1)}, bf16[127,2048]{1,0:T(8,128)(2,1)S(1)}, u32[]{:S(2)}, u32[]{:S(2)}) collective-permute-start(bf16[127,2048]{1,0:T(8,128)(2,1)S(1)} %slice_bitcast_fusion.1), channel_id=1, source_target_pairs={{0,4},{4,8},{8,12},{12,16},{16,20},{20,24},{24,28},{1,5},{5,9},{9,... | collective-permute-start | bytes 1560584 | tf_op jit(solution)/shard_map/ppermute | solution.py:14
  261.2 2.4 copy-start.2
  286.6 0.7 copy-start.3
  286.6 120.4 %copy-start.4 = (u32[32]{0:T(128)S(1)}, u32[32]{0:T(128)}, u32[]{:S(2)}) copy-start(u32[32]{0:T(128)} %constant.14) | copy-start | bytes 388
  286.6 174.4 %all-reduce.4.cloned.1.call-start = ((), (), s32[]{:S(2)}) async-start(), calls=%async_computation.3 | async-start | bytes 262144
Sparse Core Ops, SparseCore 0:
  9.9 163.4 all-gather.1
  286.8 117.7 reduce-scatter.1
  407.6 53.4 all-reduce.3
where the time goes:
time: 469 us
  local copies, waits for them, and re-layouts  220 us (47%)
  waiting for transfers between devices  172 us (37%)
  matrix products  45.9 us (10%)
  between operations  14.5 us (3%)
  other arithmetic  10.6 us (2%)
  starting transfers between devices  6.76 us (1%)
    reduce_scatter x1, waiting for transfers between devices, on_device(): lax.psum_scatter(terms.astype(jnp.bfloat16), 'tensor', scatter_dimension=...  117 us
    reshape x1, local copies, waits for them, and re-layouts, banded_filters(): return tiled[:, :rows * span].reshape(local_groups, rows, span)  106 us
    unnamed x4, waiting for transfers between devices  53.5 us
    unnamed x15, local copies, waits for them, and re-layouts  49.4 us
    slice x1, local copies, waits for them, and re-layouts, banded_filters(): return tiled[:, :rows * span].reshape(local_groups, rows, span)  36.1 us
    dot_general x1, matrix products, on_device(): jnp.dot(gated, lax.all_gather(out_weight, 'context', axis=1, tiled=True),...  23 us
    dot_general x1, matrix products, on_device(): jnp.einsum('gim,mgc->igc', toeplitz, extended.reshape(span, local_groups,...  20.4 us
    another operation x1, local copies, waits for them, and re-layouts, banded_filters(): tiled = jnp.tile(padded_taps, (1, rows))  19.8 us
  transfers between devices with their start and end apart: 5, of which 3 were waited for; matrix products, arithmetic and copies ran while one was open for 53% of the time, Pallas kernels for 0%

commit v1 on v0

--- a/solution.py
+++ b/solution.py
@@ -1,6 +1,8 @@
 import jax
 import jax.numpy as jnp
 from jax import lax
+from jax.experimental import pallas as pl
+from jax.experimental.pallas import tpu as pltpu
 from jax.sharding import PartitionSpec as P
 
 FLT = 128
@@ -75,9 +77,421 @@
     return (mixed, variant_states)
 
 
+LANES = 128
+PIECES = 4
+LAG = 2
+HALO = 144
+RIM = 16
+SLOTS = 16
+MESH = pl.DeviceIdType.MESH
+
+
+def flip(index, bit):
+    return index + bit - 2 * bit * ((index // bit) % 2)
+
+
+def arrival(step):
+    later = step - 8
+    slot = later // 4
+    way = later % 4
+    part = slot // 2
+    side = slot % 2
+    via_y = way % 2
+    mid = jnp.where(part == 1, 1, 0)
+    first = jnp.where(part == 0, 1, 0)
+    owner_x = 2 + 4 * mid
+    piece_x = side + 2 * (1 - first)
+    owner_y = 4 + 2 * mid
+    piece_y = side + 2 * first
+    owner = jnp.where(via_y == 1, owner_y, owner_x) + way // 2
+    piece = jnp.where(via_y == 1, piece_y, piece_x)
+    own = step < 8
+    return jnp.where(own, step // 4, owner), jnp.where(own, step % 4, piece)
+
+
+def fused(
+    proj, taps, bands, skip, weight, sites, mixed, picked,
+    ext, held, gated, stage, main, extra, outbox, inbox,
+    local_sem, halo_send, halo_recv, x_send, y_send, core_send, held_recv,
+    z_send, main_recv, extra_recv, pick_send, pick_recv,
+):
+    rows, width = gated.shape
+    cols = held.shape[2]
+    c = lax.axis_index("context")
+    z = lax.axis_index("tensor")
+    n_context = lax.axis_size("context")
+    n_tensor = lax.axis_size("tensor")
+    to_x, to_y, to_core = flip(c, 2), flip(c, 4), flip(c, 1)
+
+    barrier = pltpu.get_barrier_semaphore()
+    for step in range(1, n_context):
+        pl.semaphore_signal(
+            barrier, inc=1, device_id={"context": lax.rem(c + step, n_context)}, device_id_type=MESH
+        )
+
+    @pl.when(z > 0)
+    def _():
+        pl.semaphore_signal(barrier, inc=1, device_id={"tensor": z - 1}, device_id_type=MESH)
+
+    @pl.when(z < n_tensor - 1)
+    def _():
+        pl.semaphore_signal(barrier, inc=1, device_id={"tensor": z + 1}, device_id_type=MESH)
+
+    own_copies = [
+        pltpu.make_async_copy(
+            weight.at[:, pl.ds(piece * cols, cols)], held.at[piece], local_sem.at[piece]
+        )
+        for piece in range(PIECES)
+    ]
+    for copy in own_copies:
+        copy.start()
+    load = pltpu.make_async_copy(proj, ext.at[:, pl.ds(HALO, rows), :], local_sem.at[PIECES])
+    load.start()
+
+    inner = jnp.logical_and(z > 0, z < n_tensor - 1)
+    pl.semaphore_wait(barrier, n_context + jnp.where(inner, 1, 0))
+
+    def halo_copies(target):
+        return (
+            pltpu.make_async_remote_copy(
+                src_ref=proj.at[pl.ds(1, 2), pl.ds(rows - HALO, HALO), :],
+                dst_ref=ext.at[pl.ds(1, 2), pl.ds(0, HALO), :],
+                send_sem=halo_send.at[0], recv_sem=halo_recv.at[0],
+                device_id={"context": target}, device_id_type=MESH,
+            ),
+            pltpu.make_async_remote_copy(
+                src_ref=proj.at[0, pl.ds(rows - RIM, RIM), :],
+                dst_ref=ext.at[0, pl.ds(HALO - RIM, RIM), :],
+                send_sem=halo_send.at[1], recv_sem=halo_recv.at[1],
+                device_id={"context": target}, device_id_type=MESH,
+            ),
+        )
+
+    @pl.when(c < n_context - 1)
+    def _():
+        for copy in halo_copies(c + 1):
+            copy.start()
+
+    def send_held(source, landing, send_sem, target):
+        return pltpu.make_async_remote_copy(
+            src_ref=held.at[source], dst_ref=held.at[landing],
+            send_sem=send_sem, recv_sem=held_recv.at[landing],
+            device_id={"context": target}, device_id_type=MESH,
+        )
+
+    for copy in own_copies:
+        copy.wait()
+    for piece in (0, 1):
+        send_held(piece, 2 * PIECES + piece, x_send.at[piece], to_x).start()
+        send_held(piece + 2, 4 * PIECES + piece + 2, y_send.at[piece + 2], to_y).start()
+    for piece in range(PIECES):
+        send_held(piece, PIECES + piece, core_send.at[piece], to_core).start()
+
+    load.wait()
+
+    @pl.when(c == 0)
+    def _():
+        ext[:, pl.ds(0, HALO), :] = jnp.zeros((3, HALO, width), ext.dtype)
+
+    @pl.when(c > 0)
+    def _():
+        for copy in halo_copies(c):
+            copy.wait_recv()
+
+    blocks = rows // FLT
+    per_tile = LANES // GROUP
+
+    @pl.loop(0, width // LANES)
+    def _(tile):
+        lanes = pl.ds(pl.multiple_of(tile * LANES, LANES), LANES)
+
+        def feature(which, start):
+            values = ext[which, pl.ds(start - RIM, HALO + rows - start + RIM), lanes].astype(jnp.float32)
+            count = values.shape[0] - RIM
+            weights = taps[which, :, lanes]
+            total = weights[0:1] * values[RIM:]
+            for lag in range(1, SHORT):
+                total = total + weights[lag : lag + 1] * values[RIM - lag : RIM - lag + count]
+            return total
+
+        query = feature(0, HALO)
+        product = (feature(1, RIM) * feature(2, RIM)).astype(jnp.bfloat16)
+        wide = jnp.concatenate(
+            [product[b * FLT : (b + 2) * FLT] for b in range(blocks)], axis=1
+        )
+        group_of = lax.broadcasted_iota(jnp.int32, (FLT, blocks * LANES), 1) % LANES // GROUP
+        total = jnp.zeros((FLT, blocks * LANES), jnp.float32)
+        for g in range(per_tile):
+            row = bands[pl.ds(tile * per_tile + g, 1), :]
+            band = pltpu.roll(
+                jnp.broadcast_to(row, (FLT, 2 * FLT)), 0, 1, stride=1, stride_axis=0
+            ).astype(jnp.bfloat16)
+            term = jnp.dot(band, wide, preferred_element_type=jnp.float32)
+            total = jnp.where(group_of == g, term, total)
+        direct = skip[:, lanes]
+        for b in range(blocks):
+            here = product[(b + 1) * FLT : (b + 2) * FLT].astype(jnp.float32)
+            conv = total[:, b * LANES : (b + 1) * LANES] + direct * here
+            gated[pl.ds(b * FLT, FLT), lanes] = (
+                query[b * FLT : (b + 1) * FLT] * conv
+            ).astype(jnp.bfloat16)
+
+    def place(owner, piece):
+        up_y = (c // 4 + owner // 4) % 2
+        up_x = (c // 2 + owner // 2) % 2
+        up_core = (c + owner) % 2
+        return owner * PIECES + piece, 2 * up_y + up_x, up_core * PIECES + piece
+
+    def up_copy(slot):
+        return pltpu.make_async_remote_copy(
+            src_ref=stage.at[slot], dst_ref=main.at[slot],
+            send_sem=z_send.at[slot], recv_sem=main_recv.at[slot],
+            device_id={"tensor": z + 1}, device_id_type=MESH,
+        )
+
+    def down_copy(slot):
+        return pltpu.make_async_remote_copy(
+            src_ref=stage.at[slot], dst_ref=main.at[slot],
+            send_sem=z_send.at[slot], recv_sem=main_recv.at[slot],
+            device_id={"tensor": z - 1}, device_id_type=MESH,
+        )
+
+    def last_copy(slot, block):
+        return pltpu.make_async_remote_copy(
+            src_ref=stage.at[slot], dst_ref=extra.at[block],
+            send_sem=z_send.at[slot], recv_sem=extra_recv.at[block],
+            device_id={"tensor": z - 1}, device_id_type=MESH,
+        )
+
+    def pass_on(slot, goal, block):
+        @pl.when(goal > z)
+        def _():
+            up_copy(slot).start()
+
+        @pl.when(goal < z - 1)
+        def _():
+            down_copy(slot).start()
+
+        @pl.when(goal == z - 1)
+        def _():
+            last_copy(slot, block).start()
+
+    def depth(goal):
+        last = n_tensor - 1
+        return jnp.where(
+            goal > z, z, jnp.where(goal < z, last - z, jnp.maximum(z, last - z))
+        )
+
+    steps = n_context * PIECES
+
+    @pl.loop(0, steps + LAG * (n_tensor - 1))
+    def _(step):
+        @pl.when(step < steps)
+        def _():
+            owner, piece = arrival(step)
+            slot, goal, block = place(owner, piece)
+
+            @pl.when(owner > 0)
+            def _():
+                send_held(slot, slot, core_send.at[0], to_core).wait_recv()
+
+            @pl.when(jnp.logical_and(owner > 0, owner % 2 == 0))
+            def _():
+                send_held(slot, slot + PIECES, core_send.at[owner // 2 * PIECES + piece], to_core).start()
+
+            @pl.when(jnp.logical_and(owner == 2, piece < 2))
+            def _():
+                send_held(slot, 6 * PIECES + piece, y_send.at[PIECES + piece], to_y).start()
+
+            @pl.when(jnp.logical_and(owner == 4, piece >= 2))
+            def _():
+                send_held(slot, 6 * PIECES + piece, x_send.at[PIECES + piece - 2], to_x).start()
+
+            @pl.when(jnp.logical_and(owner == 2, piece == 1))
+            def _():
+                for late in (0, 1):
+                    send_held(late, 4 * PIECES + late, y_send.at[late], to_y).start()
+
+            @pl.when(jnp.logical_and(owner == 4, piece == 3))
+            def _():
+                for late in (2, 3):
+                    send_held(late, 2 * PIECES + late, x_send.at[late], to_x).start()
+
+            stage[slot] = jnp.dot(
+                gated[...], held[slot], preferred_element_type=jnp.float32
+            ).astype(jnp.bfloat16)
+
+            @pl.when(depth(goal) == 0)
+            def _():
+                pass_on(slot, goal, block)
+
+        for hop in range(1, n_tensor):
+            event = step - hop * LAG
+            owner, piece = arrival(event)
+            slot, goal, block = place(owner, piece)
+            due = jnp.logical_and(
+                jnp.logical_and(event >= 0, event < steps), depth(goal) == hop
+            )
+
+            @pl.when(jnp.logical_and(due, goal != z))
+            def _():
+                up_copy(slot).wait_recv()
+                stage[slot] = (
+                    stage[slot].astype(jnp.float32) + main[slot].astype(jnp.float32)
+                ).astype(jnp.bfloat16)
+                pass_on(slot, goal, block)
+
+            @pl.when(jnp.logical_and(due, goal == z))
+            def _():
+                spot = pl.ds(pl.multiple_of(block * cols, cols), cols)
+
+                @pl.when(z == 0)
+                def _():
+                    last_copy(slot, block).wait_recv()
+                    mixed[:, spot] = (
+                        stage[slot].astype(jnp.float32) + extra[block].astype(jnp.float32)
+                    ).astype(jnp.bfloat16)
+
+                @pl.when(z == n_tensor - 1)
+                def _():
+                    up_copy(slot).wait_recv()
+                    mixed[:, spot] = (
+                        stage[slot].astype(jnp.float32) + main[slot].astype(jnp.float32)
+                    ).astype(jnp.bfloat16)
+
+                @pl.when(jnp.logical_and(z > 0, z < n_tensor - 1))
+                def _():
+                    up_copy(slot).wait_recv()
+                    last_copy(slot, block).wait_recv()
+                    mixed[:, spot] = (
+                        stage[slot].astype(jnp.float32)
+                        + main[slot].astype(jnp.float32)
+                        + extra[block].astype(jnp.float32)
+                    ).astype(jnp.bfloat16)
+
+    local = sites[...] - c * rows
+    one_hot = (
+        lax.broadcasted_iota(jnp.int32, (local.shape[0], rows), 1) == local
+    ).astype(jnp.float32).astype(jnp.bfloat16)
+    for part in range(width // 256):
+        spot = pl.ds(part * 256, 256)
+        outbox[:, spot] = jnp.dot(
+            one_hot, mixed[:, spot], preferred_element_type=jnp.float32
+        ).astype(jnp.bfloat16)
+
+    def pick_copy(step, target):
+        return pltpu.make_async_remote_copy(
+            src_ref=outbox.at[pl.ds(pl.multiple_of(target * SLOTS, SLOTS), SLOTS), :],
+            dst_ref=inbox.at[step - 1],
+            send_sem=pick_send.at[step - 1], recv_sem=pick_recv.at[step - 1],
+            device_id={"context": target}, device_id_type=MESH,
+        )
+
+    picks = [pick_copy(step, lax.rem(c + step, n_context)) for step in range(1, n_context)]
+    for copy in picks:
+        copy.start()
+    total = outbox[pl.ds(pl.multiple_of(c * SLOTS, SLOTS), SLOTS), :].astype(jnp.float32)
+    for step, copy in enumerate(picks):
+        copy.wait_recv()
+        total = total + inbox[step].astype(jnp.float32)
+    picked[...] = total.astype(jnp.bfloat16)
+
+    for copy in picks:
+        copy.wait_send()
+
+    @pl.when(c < n_context - 1)
+    def _():
+        for copy in halo_copies(c + 1):
+            copy.wait_send()
+
+    for index in range(6):
+        send_held(0, 0, x_send.at[index], to_x).wait_send()
+        send_held(0, 0, y_send.at[index], to_y).wait_send()
+
+    @pl.loop(0, 4 * PIECES)
+    def _(index):
+        send_held(0, 0, core_send.at[index], to_core).wait_send()
+
+    @pl.loop(0, steps)
+    def _(step):
+        slot, goal, block = place(step // PIECES, step % PIECES)
+
+        @pl.when(goal != z)
+        def _():
+            up_copy(slot).wait_send()
+
+
+def fused_on_device(projected, taps, filters, skip, out_weight, positions):
+    _, rows, width = projected.shape
+    depth, mine = out_weight.shape
+    cols = mine // PIECES
+    n_context = lax.axis_size("context")
+    sites = positions.shape[0] // n_context
+    groups = filters.shape[0]
+    bands = jnp.concatenate(
+        [
+            jnp.zeros((groups, 1), filters.dtype),
+            jnp.flip(filters, axis=1),
+            jnp.zeros((groups, FLT - 1), filters.dtype),
+        ],
+        axis=1,
+    ).astype(jnp.float32)
+    padded = jnp.pad(
+        positions.reshape(n_context, sites), ((0, 0), (0, SLOTS - sites)), constant_values=-1
+    ).reshape(n_context * SLOTS, 1)
+    padded = jnp.where(padded < 0, -rows * n_context, padded)
+    chunks = n_context * PIECES
+    bf = jnp.bfloat16
+    vmem = pl.BlockSpec(memory_space=pltpu.VMEM)
+    hbm = pl.BlockSpec(memory_space=pl.ANY)
+    dma = pltpu.SemaphoreType.DMA
+    mixed, picked = pl.pallas_call(
+        fused,
+        out_shape=(
+            jax.ShapeDtypeStruct((rows, 2 * mine), bf),
+            jax.ShapeDtypeStruct((SLOTS, 2 * mine), bf),
+        ),
+        in_specs=[hbm, vmem, vmem, vmem, hbm, vmem],
+        out_specs=(vmem, vmem),
+        scratch_shapes=[
+            pltpu.VMEM((3, HALO + rows, width), bf),
+            pltpu.VMEM((chunks, depth, cols), bf),
+            pltpu.VMEM((rows, width), bf),
+            pltpu.VMEM((chunks, rows, cols), bf),
+            pltpu.VMEM((chunks, rows, cols), bf),
+            pltpu.VMEM((2 * PIECES, rows, cols), bf),
+            pltpu.VMEM((n_context * SLOTS, 2 * mine), bf),
+            pltpu.VMEM((n_context - 1, SLOTS, 2 * mine), bf),
+            dma((PIECES + 1,)),
+            dma((2,)),
+            dma((2,)),
+            dma((6,)),
+            dma((6,)),
+            dma((4 * PIECES,)),
+            dma((chunks,)),
+            dma((chunks,)),
+            dma((chunks,)),
+            dma((2 * PIECES,)),
+            dma((n_context - 1,)),
+            dma((n_context - 1,)),
+        ],
+        compiler_params=pltpu.CompilerParams(
+            collective_id=0, has_side_effects=True, vmem_limit_bytes=62 * 1024 * 1024
+        ),
+        cost_estimate=pl.CostEstimate(
+            flops=2 * rows * width * mine * n_context, bytes_accessed=2**24, transcendentals=0
+        ),
+    )(projected, taps, bands, skip.reshape(1, width), out_weight, padded)
+    return mixed, picked[:sites]
+
+
+def fits(mesh):
+    return mesh.shape["context"] == 8 and mesh.shape["tensor"] == 4
+
+
 def solution(mesh):
     return jax.shard_map(
-        on_device,
+        fused_on_device if fits(mesh) else on_device,
         mesh=mesh,
         in_specs=(
             P(None, "context", "tensor"),

time: 469 us -> 201 us (0.43)
  the two profiles are of different devices: /device:TPU:0 before, /device:TPU:13 now
where the time goes in v1:
time: 201 us; the launch traced here: 200 us
  Pallas kernels  192 us (96%)
  local copies, waits for them, and re-layouts  5.85 us (3%)
    pallas_call x1, Pallas kernels, fused_on_device(): pl.pallas_call(fused, out_shape=(jax.ShapeDtypeStruct((rows, 2 * mine), b...  192 us

profile of v1, /device:TPU:13, one launch (start us, length us, event | category | flops | bytes accessed | tf_op | source)
XLA Modules:
  0.0 200.2 jit_solution(13970973001028146145)
XLA Ops:
  0.7 0.1 pad.7.clone
  0.7 0.7 reshape.38
  1.5 0.8 rev.4
  2.3 0.1 reshape.40
  2.4 0.6 compare_select_fusion.sites
  3.0 0.7 maximum_convert_fusion.bands
  3.8 192.3 %shard_map.77 = (bf16[384,2048]{1,0:T(8,128)(2,1)}, bf16[16,2048]{1,0:T(8,128)(2,1)}) custom-call(bf16[3,384,2048]{2,1,0:T(8,128)(2,1)} %proj.1, f32[3,3,2048]{2,1,0:T(4,128)} %taps.1, f32[128,256]{1,0:T(8,128)} %maximum_convert_fusion.bands, f32[1,2048]{1,0:T(1,128)} %bitcast.2, bf16[2048,1024]{1,0:T(8,128)(2,1)} %weight.1, s32[128,1]{1,0:T(8,128)} %compare_select_fusion.sites), custom_call_target="tpu_custom_call" | custom-call | flops 12884901888 | bytes 16777216 | tf_op jit(solution)/shard_map/pallas_call | solution.py:448
  196.1 1.4 slice.3
  197.5 2.7 %copy.13 = bf16[384,2048]{1,0:T(8,128)(2,1)} copy(bf16[384,2048]{1,0:T(8,128)(2,1)} %get-tuple-element.8) | data formatting | bytes 3145728
  (3 shorter events, 0.0 us)

commit v2 on v1

--- a/solution.py
+++ b/solution.py
@@ -78,7 +78,7 @@
 
 
 LANES = 128
-PIECES = 4
+PIECES = 2
 LAG = 2
 HALO = 144
 RIM = 16
@@ -91,37 +91,48 @@
 
 
 def arrival(step):
-    later = step - 8
-    slot = later // 4
-    way = later % 4
-    part = slot // 2
-    side = slot % 2
-    via_y = way % 2
-    mid = jnp.where(part == 1, 1, 0)
-    first = jnp.where(part == 0, 1, 0)
-    owner_x = 2 + 4 * mid
-    piece_x = side + 2 * (1 - first)
-    owner_y = 4 + 2 * mid
-    piece_y = side + 2 * first
-    owner = jnp.where(via_y == 1, owner_y, owner_x) + way // 2
-    piece = jnp.where(via_y == 1, piece_y, piece_x)
-    own = step < 8
-    return jnp.where(own, step // 4, owner), jnp.where(own, step % 4, piece)
+    early = step - 4
+    round_one = step - 14
+    round_two = step - 24
+    first = step < 4
+    swapped = step < 12
+    relayed = step < 14
+    ahead = step < 22
+    tail = step < 24
+    mixed_one = 2 * (round_one % 4) + round_one // 4
+    mixed_two = 2 * (round_two % 4) + round_two // 4
+    owner = jnp.where(
+        first, step // 2,
+        jnp.where(
+            swapped, 2 + 2 * (early % 2) + early % 4 // 2,
+            jnp.where(
+                relayed, step - 6,
+                jnp.where(ahead, mixed_one, jnp.where(tail, step - 16, mixed_two)),
+            ),
+        ),
+    )
+    piece = jnp.where(
+        first, step % 2, jnp.where(swapped, early // 4, jnp.where(ahead, 0, 1))
+    )
+    late = jnp.where(relayed, 0, jnp.where(ahead, 1, jnp.where(tail, 0, 1)))
+    return owner, piece, late
 
 
 def fused(
     proj, taps, bands, skip, weight, sites, mixed, picked,
-    ext, held, gated, stage, main, extra, outbox, inbox,
+    ext, held, away, gated, stage, main, extra, outbox, inbox,
     local_sem, halo_send, halo_recv, x_send, y_send, core_send, held_recv,
     z_send, main_recv, extra_recv, pick_send, pick_recv,
+    rows_send, rows_recv, out_send, out_recv,
 ):
-    rows, width = gated.shape
+    _, rows, width = gated.shape
     cols = held.shape[2]
     c = lax.axis_index("context")
     z = lax.axis_index("tensor")
     n_context = lax.axis_size("context")
     n_tensor = lax.axis_size("tensor")
     to_x, to_y, to_core = flip(c, 2), flip(c, 4), flip(c, 1)
+    half = c // 2 % 2
 
     barrier = pltpu.get_barrier_semaphore()
     for step in range(1, n_context):
@@ -137,15 +148,26 @@
     def _():
         pl.semaphore_signal(barrier, inc=1, device_id={"tensor": z + 1}, device_id_type=MESH)
 
+    def weight_piece(side, piece):
+        return weight.at[
+            :, pl.ds(pl.multiple_of((side * PIECES + piece) * cols, cols), cols)
+        ]
+
+    away_copies = [
+        pltpu.make_async_copy(
+            weight_piece(1 - half, piece), away.at[piece], local_sem.at[piece]
+        )
+        for piece in range(PIECES)
+    ]
     own_copies = [
         pltpu.make_async_copy(
-            weight.at[:, pl.ds(piece * cols, cols)], held.at[piece], local_sem.at[piece]
+            weight_piece(half, piece), held.at[piece], local_sem.at[PIECES + piece]
         )
         for piece in range(PIECES)
     ]
-    for copy in own_copies:
+    for copy in away_copies + own_copies:
         copy.start()
-    load = pltpu.make_async_copy(proj, ext.at[:, pl.ds(HALO, rows), :], local_sem.at[PIECES])
+    load = pltpu.make_async_copy(proj, ext.at[:, pl.ds(HALO, rows), :], local_sem.at[2 * PIECES])
     load.start()
 
     inner = jnp.logical_and(z > 0, z < n_tensor - 1)
@@ -179,11 +201,18 @@
             device_id={"context": target}, device_id_type=MESH,
         )
 
-    for copy in own_copies:
-        copy.wait()
-    for piece in (0, 1):
-        send_held(piece, 2 * PIECES + piece, x_send.at[piece], to_x).start()
-        send_held(piece + 2, 4 * PIECES + piece + 2, y_send.at[piece + 2], to_y).start()
+    def send_away(piece):
+        return pltpu.make_async_remote_copy(
+            src_ref=away.at[piece], dst_ref=held.at[2 * PIECES + piece],
+            send_sem=x_send.at[piece], recv_sem=held_recv.at[2 * PIECES + piece],
+            device_id={"context": to_x}, device_id_type=MESH,
+        )
+
+    for piece in range(PIECES):
+        away_copies[piece].wait()
+        send_away(piece).start()
+        own_copies[piece].wait()
+        send_held(piece, 4 * PIECES + piece, y_send.at[piece], to_y).start()
     for piece in range(PIECES):
         send_held(piece, PIECES + piece, core_send.at[piece], to_core).start()
 
@@ -232,15 +261,38 @@
         for b in range(blocks):
             here = product[(b + 1) * FLT : (b + 2) * FLT].astype(jnp.float32)
             conv = total[:, b * LANES : (b + 1) * LANES] + direct * here
-            gated[pl.ds(b * FLT, FLT), lanes] = (
+            gated[0, pl.ds(b * FLT, FLT), lanes] = (
                 query[b * FLT : (b + 1) * FLT] * conv
             ).astype(jnp.bfloat16)
 
-    def place(owner, piece):
+    rows_copy = pltpu.make_async_remote_copy(
+        src_ref=gated.at[0], dst_ref=gated.at[1],
+        send_sem=rows_send.at[0], recv_sem=rows_recv.at[0],
+        device_id={"context": to_x}, device_id_type=MESH,
+    )
+    rows_copy.start()
+
+    def place(owner, piece, late):
         up_y = (c // 4 + owner // 4) % 2
         up_x = (c // 2 + owner // 2) % 2
         up_core = (c + owner) % 2
-        return owner * PIECES + piece, 2 * up_y + up_x, up_core * PIECES + piece
+        slot = (late * n_context + owner) * PIECES + piece
+        block = (late * 2 + up_core) * PIECES + piece
+        return slot, 2 * up_y + up_x, block
+
+    def spot_of(block, side):
+        core = block // PIECES % 2
+        index = (core * 2 + side) * PIECES + block % PIECES
+        return pl.ds(pl.multiple_of(index * cols, cols), cols)
+
+    def out_copy(slot, block):
+        spot = spot_of(block, half)
+        lane = block % (2 * PIECES)
+        return pltpu.make_async_remote_copy(
+            src_ref=stage.at[slot], dst_ref=mixed.at[:, spot],
+            send_sem=out_send.at[lane], recv_sem=out_recv.at[lane],
+            device_id={"context": to_x}, device_id_type=MESH,
+        )
 
     def up_copy(slot):
         return pltpu.make_async_remote_copy(
@@ -282,43 +334,36 @@
             goal > z, z, jnp.where(goal < z, last - z, jnp.maximum(z, last - z))
         )
 
-    steps = n_context * PIECES
+    steps = 2 * n_context * PIECES
 
     @pl.loop(0, steps + LAG * (n_tensor - 1))
     def _(step):
         @pl.when(step < steps)
         def _():
-            owner, piece = arrival(step)
-            slot, goal, block = place(owner, piece)
-
-            @pl.when(owner > 0)
-            def _():
-                send_held(slot, slot, core_send.at[0], to_core).wait_recv()
-
-            @pl.when(jnp.logical_and(owner > 0, owner % 2 == 0))
-            def _():
-                send_held(slot, slot + PIECES, core_send.at[owner // 2 * PIECES + piece], to_core).start()
-
-            @pl.when(jnp.logical_and(owner == 2, piece < 2))
-            def _():
-                send_held(slot, 6 * PIECES + piece, y_send.at[PIECES + piece], to_y).start()
-
-            @pl.when(jnp.logical_and(owner == 4, piece >= 2))
-            def _():
-                send_held(slot, 6 * PIECES + piece, x_send.at[PIECES + piece - 2], to_x).start()
-
-            @pl.when(jnp.logical_and(owner == 2, piece == 1))
-            def _():
-                for late in (0, 1):
-                    send_held(late, 4 * PIECES + late, y_send.at[late], to_y).start()
-
-            @pl.when(jnp.logical_and(owner == 4, piece == 3))
-            def _():
-                for late in (2, 3):
-                    send_held(late, 2 * PIECES + late, x_send.at[late], to_x).start()
+            owner, piece, late = arrival(step)
+            slot, goal, block = place(owner, piece, late)
+            chunk = owner * PIECES + piece
+
+            @pl.when(jnp.logical_and(late == 0, owner > 0))
+            def _():
+                send_held(chunk, chunk, core_send.at[0], to_core).wait_recv()
+
+            @pl.when(jnp.logical_and(late == 0, jnp.logical_and(owner > 0, owner % 2 == 0)))
+            def _():
+                send_held(
+                    chunk, chunk + PIECES, core_send.at[owner // 2 * PIECES + piece], to_core
+                ).start()
+
+            @pl.when(jnp.logical_and(late == 0, owner == 2))
+            def _():
+                send_held(chunk, 6 * PIECES + piece, y_send.at[PIECES + piece], to_y).start()
+
+            @pl.when(step == 14)
+            def _():
+                rows_copy.wait_recv()
 
             stage[slot] = jnp.dot(
-                gated[...], held[slot], preferred_element_type=jnp.float32
+                gated[late], held[chunk], preferred_element_type=jnp.float32
             ).astype(jnp.bfloat16)
 
             @pl.when(depth(goal) == 0)
@@ -327,8 +372,8 @@
 
         for hop in range(1, n_tensor):
             event = step - hop * LAG
-            owner, piece = arrival(event)
-            slot, goal, block = place(owner, piece)
+            owner, piece, late = arrival(event)
+            slot, goal, block = place(owner, piece, late)
             due = jnp.logical_and(
                 jnp.logical_and(event >= 0, event < steps), depth(goal) == hop
             )
@@ -343,31 +388,50 @@
 
             @pl.when(jnp.logical_and(due, goal == z))
             def _():
-                spot = pl.ds(pl.multiple_of(block * cols, cols), cols)
+                @pl.when(z < n_tensor - 1)
+                def _():
+                    last_copy(slot, block).wait_recv()
+
+                @pl.when(z > 0)
+                def _():
+                    up_copy(slot).wait_recv()
+
+                def finish(result):
+                    @pl.when(late == 0)
+                    def _():
+                        mixed[:, spot_of(block, half)] = result
+
+                    @pl.when(late == 1)
+                    def _():
+                        stage[slot] = result
+                        out_copy(slot, block).start()
 
                 @pl.when(z == 0)
                 def _():
-                    last_copy(slot, block).wait_recv()
-                    mixed[:, spot] = (
+                    finish((
                         stage[slot].astype(jnp.float32) + extra[block].astype(jnp.float32)
-                    ).astype(jnp.bfloat16)
+                    ).astype(jnp.bfloat16))
 
                 @pl.when(z == n_tensor - 1)
                 def _():
-                    up_copy(slot).wait_recv()
-                    mixed[:, spot] = (
+                    finish((
                         stage[slot].astype(jnp.float32) + main[slot].astype(jnp.float32)
-                    ).astype(jnp.bfloat16)
+                    ).astype(jnp.bfloat16))
 
                 @pl.when(jnp.logical_and(z > 0, z < n_tensor - 1))
                 def _():
-                    up_copy(slot).wait_recv()
-                    last_copy(slot, block).wait_recv()
-                    mixed[:, spot] = (
+                    finish((
                         stage[slot].astype(jnp.float32)
                         + main[slot].astype(jnp.float32)
                         + extra[block].astype(jnp.float32)
-                    ).astype(jnp.bfloat16)
+                    ).astype(jnp.bfloat16))
+
+    for lane in range(2 * PIECES):
+        pltpu.make_async_remote_copy(
+            src_ref=stage.at[0], dst_ref=mixed.at[:, spot_of(lane, 1 - half)],
+            send_sem=out_send.at[lane], recv_sem=out_recv.at[lane],
+            device_id={"context": to_x}, device_id_type=MESH,
+        ).wait_recv()
 
     local = sites[...] - c * rows
     one_hot = (
@@ -404,9 +468,12 @@
         for copy in halo_copies(c + 1):
             copy.wait_send()
 
-    for index in range(6):
-        send_held(0, 0, x_send.at[index], to_x).wait_send()
+    rows_copy.wait_send()
+    for piece in range(PIECES):
+        send_away(piece).wait_send()
+    for index in range(2 * PIECES):
         send_held(0, 0, y_send.at[index], to_y).wait_send()
+        out_copy(0, index).wait_send()
 
     @pl.loop(0, 4 * PIECES)
     def _(index):
@@ -414,7 +481,8 @@
 
     @pl.loop(0, steps)
     def _(step):
-        slot, goal, block = place(step // PIECES, step % PIECES)
+        owner, piece, late = arrival(step)
+        slot, goal, block = place(owner, piece, late)
 
         @pl.when(goal != z)
         def _():
@@ -424,7 +492,7 @@
 def fused_on_device(projected, taps, filters, skip, out_weight, positions):
     _, rows, width = projected.shape
     depth, mine = out_weight.shape
-    cols = mine // PIECES
+    cols = mine // (2 * PIECES)
     n_context = lax.axis_size("context")
     sites = positions.shape[0] // n_context
     groups = filters.shape[0]
@@ -456,24 +524,29 @@
         scratch_shapes=[
             pltpu.VMEM((3, HALO + rows, width), bf),
             pltpu.VMEM((chunks, depth, cols), bf),
-            pltpu.VMEM((rows, width), bf),
-            pltpu.VMEM((chunks, rows, cols), bf),
-            pltpu.VMEM((chunks, rows, cols), bf),
-            pltpu.VMEM((2 * PIECES, rows, cols), bf),
+            pltpu.VMEM((PIECES, depth, cols), bf),
+            pltpu.VMEM((2, rows, width), bf),
+            pltpu.VMEM((2 * chunks, rows, cols), bf),
+            pltpu.VMEM((2 * chunks, rows, cols), bf),
+            pltpu.VMEM((4 * PIECES, rows, cols), bf),
             pltpu.VMEM((n_context * SLOTS, 2 * mine), bf),
             pltpu.VMEM((n_context - 1, SLOTS, 2 * mine), bf),
-            dma((PIECES + 1,)),
+            dma((2 * PIECES + 1,)),
             dma((2,)),
             dma((2,)),
-            dma((6,)),
-            dma((6,)),
+            dma((PIECES,)),
+            dma((2 * PIECES,)),
             dma((4 * PIECES,)),
             dma((chunks,)),
-            dma((chunks,)),
-            dma((chunks,)),
-            dma((2 * PIECES,)),
+            dma((2 * chunks,)),
+            dma((2 * chunks,)),
+            dma((4 * PIECES,)),
             dma((n_context - 1,)),
             dma((n_context - 1,)),
+            dma((1,)),
+            dma((1,)),
+            dma((2 * PIECES,)),
+            dma((2 * PIECES,)),
         ],
         compiler_params=pltpu.CompilerParams(
             collective_id=0, has_side_effects=True, vmem_limit_bytes=62 * 1024 * 1024

time: 201 us -> 198 us (0.985)
  the two profiles are of different devices: /device:TPU:13 before, /device:TPU:0 now
where the time goes in v2:
time: 198 us
  Pallas kernels  190 us (96%)
  local copies, waits for them, and re-layouts  5.85 us (3%)
    pallas_call x1, Pallas kernels, fused_on_device(): pl.pallas_call(fused, out_shape=(jax.ShapeDtypeStruct((rows, 2 * mine), b...  190 us

profile of v2, /device:TPU:0, one launch (start us, length us, event | category | flops | bytes accessed | tf_op | source)
XLA Modules:
  0.0 197.6 jit_solution(15550475084334414047)
XLA Ops:
  0.7 0.1 pad.7.clone
  0.7 0.7 reshape.38
  1.5 0.8 rev.4
  2.3 0.1 reshape.40
  2.4 0.6 compare_select_fusion.sites
  3.0 0.7 maximum_convert_fusion.bands
  3.8 189.7 %shard_map.77 = (bf16[384,2048]{1,0:T(8,128)(2,1)}, bf16[16,2048]{1,0:T(8,128)(2,1)}) custom-call(bf16[3,384,2048]{2,1,0:T(8,128)(2,1)} %proj.1, f32[3,3,2048]{2,1,0:T(4,128)} %taps.1, f32[128,256]{1,0:T(8,128)} %maximum_convert_fusion.bands, f32[1,2048]{1,0:T(1,128)} %bitcast.2, bf16[2048,1024]{1,0:T(8,128)(2,1)} %weight.1, s32[128,1]{1,0:T(8,128)} %compare_select_fusion.sites), custom_call_target="tpu_custom_call" | custom-call | flops 12884901888 | bytes 16777216 | tf_op jit(solution)/shard_map/pallas_call | solution.py:516
  193.5 1.4 slice.3
  194.9 2.7 %copy.13 = bf16[384,2048]{1,0:T(8,128)(2,1)} copy(bf16[384,2048]{1,0:T(8,128)(2,1)} %get-tuple-element.8) | data formatting | bytes 3145728
  (3 shorter events, 0.0 us)

commit v3 on v2

--- a/solution.py
+++ b/solution.py
@@ -79,7 +79,7 @@
 
 LANES = 128
 PIECES = 2
-LAG = 2
+LAG = 3
 HALO = 144
 RIM = 16
 SLOTS = 16
@@ -119,8 +119,8 @@
 
 
 def fused(
-    proj, taps, bands, skip, weight, sites, mixed, picked,
-    ext, held, away, gated, stage, main, extra, outbox, inbox,
+    proj, taps, filters, skip, weight, sites, mixed, picked,
+    ext, base, bands, held, away, gated, stage, main, extra, outbox, inbox,
     local_sem, halo_send, halo_recv, x_send, y_send, core_send, held_recv,
     z_send, main_recv, extra_recv, pick_send, pick_recv,
     rows_send, rows_recv, out_send, out_recv,
@@ -194,6 +194,21 @@
         for copy in halo_copies(c + 1):
             copy.start()
 
+    shape = (FLT, 2 * FLT)
+    mirror = (
+        lax.broadcasted_iota(jnp.int32, shape, 0) + lax.broadcasted_iota(jnp.int32, shape, 1) == FLT
+    ).astype(jnp.float32).astype(jnp.bfloat16)
+    base[...] = jnp.dot(filters[...], mirror, preferred_element_type=jnp.float32)
+
+    @pl.loop(0, filters.shape[0] // 8)
+    def _(octet):
+        taken = base[pl.ds(pl.multiple_of(octet * 8, 8), 8), :]
+        for g in range(8):
+            row = jnp.broadcast_to(taken[g : g + 1], shape)
+            bands[octet * 8 + g] = pltpu.roll(row, 0, 1, stride=1, stride_axis=0).astype(
+                jnp.bfloat16
+            )
+
     def send_held(source, landing, send_sem, target):
         return pltpu.make_async_remote_copy(
             src_ref=held.at[source], dst_ref=held.at[landing],
@@ -251,10 +266,7 @@
         group_of = lax.broadcasted_iota(jnp.int32, (FLT, blocks * LANES), 1) % LANES // GROUP
         total = jnp.zeros((FLT, blocks * LANES), jnp.float32)
         for g in range(per_tile):
-            row = bands[pl.ds(tile * per_tile + g, 1), :]
-            band = pltpu.roll(
-                jnp.broadcast_to(row, (FLT, 2 * FLT)), 0, 1, stride=1, stride_axis=0
-            ).astype(jnp.bfloat16)
+            band = bands[tile * per_tile + g]
             term = jnp.dot(band, wide, preferred_element_type=jnp.float32)
             total = jnp.where(group_of == g, term, total)
         direct = skip[:, lanes]
@@ -433,9 +445,16 @@
             device_id={"context": to_x}, device_id_type=MESH,
         ).wait_recv()
 
-    local = sites[...] - c * rows
+    count = sites.shape[0]
+    each = count // n_context
+    row_at = lax.broadcasted_iota(jnp.int32, (n_context * SLOTS, 1), 0)
+    local = jnp.full((n_context * SLOTS, 1), -1, jnp.int32)
+    for v in range(count):
+        local = jnp.where(
+            row_at == v // each * SLOTS + v % each, sites[v] - c * rows, local
+        )
     one_hot = (
-        lax.broadcasted_iota(jnp.int32, (local.shape[0], rows), 1) == local
+        lax.broadcasted_iota(jnp.int32, (n_context * SLOTS, rows), 1) == local
     ).astype(jnp.float32).astype(jnp.bfloat16)
     for part in range(width // 256):
         spot = pl.ds(part * 256, 256)
@@ -458,7 +477,7 @@
     for step, copy in enumerate(picks):
         copy.wait_recv()
         total = total + inbox[step].astype(jnp.float32)
-    picked[...] = total.astype(jnp.bfloat16)
+    picked[...] = total[:each].astype(jnp.bfloat16)
 
     for copy in picks:
         copy.wait_send()
@@ -496,18 +515,6 @@
     n_context = lax.axis_size("context")
     sites = positions.shape[0] // n_context
     groups = filters.shape[0]
-    bands = jnp.concatenate(
-        [
-            jnp.zeros((groups, 1), filters.dtype),
-            jnp.flip(filters, axis=1),
-            jnp.zeros((groups, FLT - 1), filters.dtype),
-        ],
-        axis=1,
-    ).astype(jnp.float32)
-    padded = jnp.pad(
-        positions.reshape(n_context, sites), ((0, 0), (0, SLOTS - sites)), constant_values=-1
-    ).reshape(n_context * SLOTS, 1)
-    padded = jnp.where(padded < 0, -rows * n_context, padded)
     chunks = n_context * PIECES
     bf = jnp.bfloat16
     vmem = pl.BlockSpec(memory_space=pltpu.VMEM)
@@ -517,12 +524,16 @@
         fused,
         out_shape=(
             jax.ShapeDtypeStruct((rows, 2 * mine), bf),
-            jax.ShapeDtypeStruct((SLOTS, 2 * mine), bf),
+            jax.ShapeDtypeStruct((sites, 2 * mine), bf),
         ),
-        in_specs=[hbm, vmem, vmem, vmem, hbm, vmem],
+        in_specs=[
+            hbm, vmem, vmem, vmem, hbm, pl.BlockSpec(memory_space=pltpu.SMEM)
+        ],
         out_specs=(vmem, vmem),
         scratch_shapes=[
             pltpu.VMEM((3, HALO + rows, width), bf),
+            pltpu.VMEM((groups, 2 * FLT), jnp.float32),
+            pltpu.VMEM((groups, FLT, 2 * FLT), bf),
             pltpu.VMEM((chunks, depth, cols), bf),
             pltpu.VMEM((PIECES, depth, cols), bf),
             pltpu.VMEM((2, rows, width), bf),
@@ -554,8 +565,8 @@
         cost_estimate=pl.CostEstimate(
             flops=2 * rows * width * mine * n_context, bytes_accessed=2**24, transcendentals=0
         ),
-    )(projected, taps, bands, skip.reshape(1, width), out_weight, padded)
-    return mixed, picked[:sites]
+    )(projected, taps, filters, skip.reshape(1, width), out_weight, positions)
+    return mixed, picked
 
 
 def fits(mesh):

time: 198 us -> 187 us (0.944)
  Pallas kernels: 190 us -> 181 us
    pallas_call x1, Pallas kernels: 190 us -> 181 us  [fused_on_device(): pl.pallas_call(fused, out_shape=(jax.ShapeDtypeStruct((rows, 2 * mine), b...]
    unnamed x1 -> x2, local copies, waits for them, and re-layouts: 2.73 us -> 4.06 us
where the time goes in v3:
time: 187 us; the launch traced here: 186 us
  Pallas kernels  181 us (97%)
  local copies, waits for them, and re-layouts  4.06 us (2%)
    pallas_call x1, Pallas kernels, fused_on_device(): pl.pallas_call(fused, out_shape=(jax.ShapeDtypeStruct((rows, 2 * mine), b...  181 us
    unnamed x2, local copies, waits for them, and re-layouts  4.06 us

profile of v3, /device:TPU:0, one launch (start us, length us, event | category | flops | bytes accessed | tf_op | source)
XLA Modules:
  0.0 185.8 jit_solution(5013490678133177245)
XLA Ops:
  0.6 181.1 %shard_map.77 = (bf16[384,2048]{1,0:T(8,128)(2,1)}, bf16[4,2048]{1,0:T(4,128)(2,1)}) custom-call(bf16[3,384,2048]{2,1,0:T(8,128)(2,1)} %proj.1, f32[3,3,2048]{2,1,0:T(4,128)} %taps.1, bf16[128,128]{1,0:T(8,128)(2,1)} %filters.1, f32[1,2048]{1,0:T(1,128)} %bitcast.1, bf16[2048,1024]{1,0:T(8,128)(2,1)} %weight.1, s32[32]{0:T(128)} %sites.1), custom_call_target="tpu_custom_call" | custom-call | flops 12884901888 | bytes 16777216 | tf_op jit(solution)/shard_map/pallas_call | solution.py:523
  181.7 2.7 %copy.10 = bf16[384,2048]{1,0:T(8,128)(2,1)} copy(bf16[384,2048]{1,0:T(8,128)(2,1)} %get-tuple-element.4) | data formatting | bytes 3145728
  184.4 1.3 copy.11

commit v4 on v3

--- a/solution.py
+++ b/solution.py
@@ -90,32 +90,35 @@
     return index + bit - 2 * bit * ((index // bit) % 2)
 
 
+ORDER = (
+    (0, 0, 0), (0, 1, 0), (1, 0, 0), (1, 1, 0), (2, 0, 0), (4, 0, 0), (3, 0, 0), (5, 0, 0),
+    (4, 1, 0), (5, 1, 0), (0, 0, 1), (0, 1, 1), (1, 0, 1), (1, 1, 1), (2, 0, 1), (4, 0, 1),
+    (3, 0, 1), (5, 0, 1), (4, 1, 1), (5, 1, 1), (6, 0, 1), (7, 0, 1), (6, 0, 0), (7, 0, 0),
+    (2, 1, 1), (3, 1, 1), (2, 1, 0), (3, 1, 0), (6, 1, 1), (7, 1, 1), (6, 1, 0), (7, 1, 0),
+)
+ROWS_STEP = 10
+RELAY_STEP = 18
+
+
+def coded():
+    seen = {(0, 0), (0, 1), (2, 1)}
+    codes = []
+    for owner, piece, late in ORDER:
+        fresh = (owner, piece) not in seen
+        seen.add((owner, piece))
+        codes.append(owner * 8 + piece * 4 + late * 2 + int(fresh))
+    return codes
+
+
 def arrival(step):
-    early = step - 4
-    round_one = step - 14
-    round_two = step - 24
-    first = step < 4
-    swapped = step < 12
-    relayed = step < 14
-    ahead = step < 22
-    tail = step < 24
-    mixed_one = 2 * (round_one % 4) + round_one // 4
-    mixed_two = 2 * (round_two % 4) + round_two // 4
-    owner = jnp.where(
-        first, step // 2,
-        jnp.where(
-            swapped, 2 + 2 * (early % 2) + early % 4 // 2,
-            jnp.where(
-                relayed, step - 6,
-                jnp.where(ahead, mixed_one, jnp.where(tail, step - 16, mixed_two)),
-            ),
-        ),
-    )
-    piece = jnp.where(
-        first, step % 2, jnp.where(swapped, early // 4, jnp.where(ahead, 0, 1))
-    )
-    late = jnp.where(relayed, 0, jnp.where(ahead, 1, jnp.where(tail, 0, 1)))
-    return owner, piece, late
+    values = coded()
+    rest = jnp.maximum(step, 0)
+    while len(values) > 1:
+        odd = rest % 2 == 1
+        values = [jnp.where(odd, b, a) for a, b in zip(values[::2], values[1::2])]
+        rest = rest // 2
+    code = values[0]
+    return code // 8, code // 4 % 2, code // 2 % 2, code % 2
 
 
 def fused(
@@ -205,9 +208,10 @@
         taken = base[pl.ds(pl.multiple_of(octet * 8, 8), 8), :]
         for g in range(8):
             row = jnp.broadcast_to(taken[g : g + 1], shape)
-            bands[octet * 8 + g] = pltpu.roll(row, 0, 1, stride=1, stride_axis=0).astype(
-                jnp.bfloat16
-            )
+            start = pl.multiple_of((octet * 8 + g) * FLT, FLT)
+            bands[pl.ds(start, FLT), :] = pltpu.roll(
+                row, 0, 1, stride=1, stride_axis=0
+            ).astype(jnp.bfloat16)
 
     def send_held(source, landing, send_sem, target):
         return pltpu.make_async_remote_copy(
@@ -225,7 +229,8 @@
 
     for piece in range(PIECES):
         away_copies[piece].wait()
-        send_away(piece).start()
+        if piece == 0:
+            send_away(piece).start()
         own_copies[piece].wait()
         send_held(piece, 4 * PIECES + piece, y_send.at[piece], to_y).start()
     for piece in range(PIECES):
@@ -264,11 +269,13 @@
             [product[b * FLT : (b + 2) * FLT] for b in range(blocks)], axis=1
         )
         group_of = lax.broadcasted_iota(jnp.int32, (FLT, blocks * LANES), 1) % LANES // GROUP
-        total = jnp.zeros((FLT, blocks * LANES), jnp.float32)
-        for g in range(per_tile):
-            band = bands[tile * per_tile + g]
-            term = jnp.dot(band, wide, preferred_element_type=jnp.float32)
-            total = jnp.where(group_of == g, term, total)
+        start = pl.multiple_of(tile * (per_tile * FLT), per_tile * FLT)
+        terms = jnp.dot(
+            bands[pl.ds(start, per_tile * FLT), :], wide, preferred_element_type=jnp.float32
+        )
+        total = terms[:FLT]
+        for g in range(1, per_tile):
+            total = jnp.where(group_of == g, terms[g * FLT : (g + 1) * FLT], total)
         direct = skip[:, lanes]
         for b in range(blocks):
             here = product[(b + 1) * FLT : (b + 2) * FLT].astype(jnp.float32)
@@ -352,27 +359,35 @@
     def _(step):
         @pl.when(step < steps)
         def _():
-            owner, piece, late = arrival(step)
+            owner, piece, late, fresh = arrival(step)
             slot, goal, block = place(owner, piece, late)
             chunk = owner * PIECES + piece
 
-            @pl.when(jnp.logical_and(late == 0, owner > 0))
+            @pl.when(fresh == 1)
             def _():
                 send_held(chunk, chunk, core_send.at[0], to_core).wait_recv()
 
-            @pl.when(jnp.logical_and(late == 0, jnp.logical_and(owner > 0, owner % 2 == 0)))
+            @pl.when(jnp.logical_and(fresh == 1, owner % 2 == 0))
             def _():
                 send_held(
                     chunk, chunk + PIECES, core_send.at[owner // 2 * PIECES + piece], to_core
                 ).start()
 
-            @pl.when(jnp.logical_and(late == 0, owner == 2))
+            @pl.when(jnp.logical_and(fresh == 1, owner == 2))
             def _():
                 send_held(chunk, 6 * PIECES + piece, y_send.at[PIECES + piece], to_y).start()
 
-            @pl.when(step == 14)
+            @pl.when(step == RELAY_STEP)
+            def _():
+                swapped = 2 * PIECES + 1
+                send_away(1).wait_recv()
+                send_held(swapped, 6 * PIECES + 1, y_send.at[PIECES + 1], to_y).start()
+                send_held(swapped, 3 * PIECES + 1, core_send.at[PIECES + 1], to_core).start()
+
+            @pl.when(step == ROWS_STEP)
             def _():
                 rows_copy.wait_recv()
+                send_away(1).start()
 
             stage[slot] = jnp.dot(
                 gated[late], held[chunk], preferred_element_type=jnp.float32
@@ -384,7 +399,7 @@
 
         for hop in range(1, n_tensor):
             event = step - hop * LAG
-            owner, piece, late = arrival(event)
+            owner, piece, late, _ = arrival(event)
             slot, goal, block = place(owner, piece, late)
             due = jnp.logical_and(
                 jnp.logical_and(event >= 0, event < steps), depth(goal) == hop
@@ -500,7 +515,7 @@
 
     @pl.loop(0, steps)
     def _(step):
-        owner, piece, late = arrival(step)
+        owner, piece, late, _ = arrival(step)
         slot, goal, block = place(owner, piece, late)
 
         @pl.when(goal != z)
@@ -533,7 +548,7 @@
         scratch_shapes=[
             pltpu.VMEM((3, HALO + rows, width), bf),
             pltpu.VMEM((groups, 2 * FLT), jnp.float32),
-            pltpu.VMEM((groups, FLT, 2 * FLT), bf),
+            pltpu.VMEM((groups * FLT, 2 * FLT), bf),
             pltpu.VMEM((chunks, depth, cols), bf),
             pltpu.VMEM((PIECES, depth, cols), bf),
             pltpu.VMEM((2, rows, width), bf),

time: 187 us -> 187 us (level)
  no operation moved by 1% of the time
where the time goes in v4:
time: 187 us
  Pallas kernels  182 us (97%)
  local copies, waits for them, and re-layouts  4.06 us (2%)
    pallas_call x1, Pallas kernels, fused_on_device(): pl.pallas_call(fused, out_shape=(jax.ShapeDtypeStruct((rows, 2 * mine), b...  182 us
    unnamed x2, local copies, waits for them, and re-layouts  4.06 us

profile of v4, /device:TPU:0, one launch (start us, length us, event | category | flops | bytes accessed | tf_op | source)
XLA Modules:
  0.0 187.0 jit_solution(8449229546080169244)
XLA Ops:
  0.6 182.3 %shard_map.77 = (bf16[384,2048]{1,0:T(8,128)(2,1)}, bf16[4,2048]{1,0:T(4,128)(2,1)}) custom-call(bf16[3,384,2048]{2,1,0:T(8,128)(2,1)} %proj.1, f32[3,3,2048]{2,1,0:T(4,128)} %taps.1, bf16[128,128]{1,0:T(8,128)(2,1)} %filters.1, f32[1,2048]{1,0:T(1,128)} %bitcast.1, bf16[2048,1024]{1,0:T(8,128)(2,1)} %weight.1, s32[32]{0:T(128)} %sites.1), custom_call_target="tpu_custom_call" | custom-call | flops 12884901888 | bytes 16777216 | tf_op jit(solution)/shard_map/pallas_call | solution.py:538
  182.9 2.7 %copy.10 = bf16[384,2048]{1,0:T(8,128)(2,1)} copy(bf16[384,2048]{1,0:T(8,128)(2,1)} %get-tuple-element.4) | data formatting | bytes 3145728
  185.6 1.3 copy.11

commit v5 on v4

--- a/solution.py
+++ b/solution.py
@@ -94,14 +94,15 @@
     (0, 0, 0), (0, 1, 0), (1, 0, 0), (1, 1, 0), (2, 0, 0), (4, 0, 0), (3, 0, 0), (5, 0, 0),
     (4, 1, 0), (5, 1, 0), (0, 0, 1), (0, 1, 1), (1, 0, 1), (1, 1, 1), (2, 0, 1), (4, 0, 1),
     (3, 0, 1), (5, 0, 1), (4, 1, 1), (5, 1, 1), (6, 0, 1), (7, 0, 1), (6, 0, 0), (7, 0, 0),
-    (2, 1, 1), (3, 1, 1), (2, 1, 0), (3, 1, 0), (6, 1, 1), (7, 1, 1), (6, 1, 0), (7, 1, 0),
+    (2, 1, 1), (3, 1, 1), (6, 1, 1), (2, 1, 0), (7, 1, 1), (3, 1, 0), (6, 1, 0), (7, 1, 0),
 )
+EARLY = 4
 ROWS_STEP = 10
 RELAY_STEP = 18
 
 
 def coded():
-    seen = {(0, 0), (0, 1), (2, 1)}
+    seen = {(0, 0), (0, 1), (1, 0), (1, 1), (2, 1)}
     codes = []
     for owner, piece, late in ORDER:
         fresh = (owner, piece) not in seen
@@ -179,15 +180,15 @@
     def halo_copies(target):
         return (
             pltpu.make_async_remote_copy(
-                src_ref=proj.at[pl.ds(1, 2), pl.ds(rows - HALO, HALO), :],
-                dst_ref=ext.at[pl.ds(1, 2), pl.ds(0, HALO), :],
-                send_sem=halo_send.at[0], recv_sem=halo_recv.at[0],
+                src_ref=proj.at[:, pl.ds(rows - RIM, RIM), :],
+                dst_ref=ext.at[:, pl.ds(HALO - RIM, RIM), :],
+                send_sem=halo_send.at[1], recv_sem=halo_recv.at[1],
                 device_id={"context": target}, device_id_type=MESH,
             ),
             pltpu.make_async_remote_copy(
-                src_ref=proj.at[0, pl.ds(rows - RIM, RIM), :],
-                dst_ref=ext.at[0, pl.ds(HALO - RIM, RIM), :],
-                send_sem=halo_send.at[1], recv_sem=halo_recv.at[1],
+                src_ref=proj.at[pl.ds(1, 2), pl.ds(rows - HALO, HALO - RIM), :],
+                dst_ref=ext.at[pl.ds(1, 2), pl.ds(0, HALO - RIM), :],
+                send_sem=halo_send.at[0], recv_sem=halo_recv.at[0],
                 device_id={"context": target}, device_id_type=MESH,
             ),
         )
@@ -244,18 +245,17 @@
 
     @pl.when(c > 0)
     def _():
-        for copy in halo_copies(c):
-            copy.wait_recv()
+        halo_copies(c)[0].wait_recv()
 
     blocks = rows // FLT
     per_tile = LANES // GROUP
 
-    @pl.loop(0, width // LANES)
-    def _(tile):
+    def convolve(tile, low, high):
         lanes = pl.ds(pl.multiple_of(tile * LANES, LANES), LANES)
 
         def feature(which, start):
-            values = ext[which, pl.ds(start - RIM, HALO + rows - start + RIM), lanes].astype(jnp.float32)
+            stop = HALO + high * FLT
+            values = ext[which, pl.ds(start - RIM, stop - start + RIM), lanes].astype(jnp.float32)
             count = values.shape[0] - RIM
             weights = taps[which, :, lanes]
             total = weights[0:1] * values[RIM:]
@@ -263,12 +263,13 @@
                 total = total + weights[lag : lag + 1] * values[RIM - lag : RIM - lag + count]
             return total
 
-        query = feature(0, HALO)
-        product = (feature(1, RIM) * feature(2, RIM)).astype(jnp.bfloat16)
+        query = feature(0, HALO + low * FLT)
+        before = RIM + low * FLT
+        product = (feature(1, before) * feature(2, before)).astype(jnp.bfloat16)
         wide = jnp.concatenate(
-            [product[b * FLT : (b + 2) * FLT] for b in range(blocks)], axis=1
-        )
-        group_of = lax.broadcasted_iota(jnp.int32, (FLT, blocks * LANES), 1) % LANES // GROUP
+            [product[b * FLT : (b + 2) * FLT] for b in range(high - low)], axis=1
+        )
+        group_of = lax.broadcasted_iota(jnp.int32, (FLT, (high - low) * LANES), 1) % LANES // GROUP
         start = pl.multiple_of(tile * (per_tile * FLT), per_tile * FLT)
         terms = jnp.dot(
             bands[pl.ds(start, per_tile * FLT), :], wide, preferred_element_type=jnp.float32
@@ -277,19 +278,16 @@
         for g in range(1, per_tile):
             total = jnp.where(group_of == g, terms[g * FLT : (g + 1) * FLT], total)
         direct = skip[:, lanes]
-        for b in range(blocks):
+        for b in range(high - low):
             here = product[(b + 1) * FLT : (b + 2) * FLT].astype(jnp.float32)
             conv = total[:, b * LANES : (b + 1) * LANES] + direct * here
-            gated[0, pl.ds(b * FLT, FLT), lanes] = (
+            gated[0, pl.ds((low + b) * FLT, FLT), lanes] = (
                 query[b * FLT : (b + 1) * FLT] * conv
             ).astype(jnp.bfloat16)
 
-    rows_copy = pltpu.make_async_remote_copy(
-        src_ref=gated.at[0], dst_ref=gated.at[1],
-        send_sem=rows_send.at[0], recv_sem=rows_recv.at[0],
-        device_id={"context": to_x}, device_id_type=MESH,
-    )
-    rows_copy.start()
+    @pl.loop(0, width // LANES)
+    def _(tile):
+        convolve(tile, 1, blocks)
 
     def place(owner, piece, late):
         up_y = (c // 4 + owner // 4) % 2
@@ -313,45 +311,77 @@
             device_id={"context": to_x}, device_id_type=MESH,
         )
 
-    def up_copy(slot):
+    def hop_copy(slot, landing, sem, target, part):
         return pltpu.make_async_remote_copy(
-            src_ref=stage.at[slot], dst_ref=main.at[slot],
-            send_sem=z_send.at[slot], recv_sem=main_recv.at[slot],
-            device_id={"tensor": z + 1}, device_id_type=MESH,
-        )
-
-    def down_copy(slot):
-        return pltpu.make_async_remote_copy(
-            src_ref=stage.at[slot], dst_ref=main.at[slot],
-            send_sem=z_send.at[slot], recv_sem=main_recv.at[slot],
-            device_id={"tensor": z - 1}, device_id_type=MESH,
-        )
-
-    def last_copy(slot, block):
-        return pltpu.make_async_remote_copy(
-            src_ref=stage.at[slot], dst_ref=extra.at[block],
-            send_sem=z_send.at[slot], recv_sem=extra_recv.at[block],
-            device_id={"tensor": z - 1}, device_id_type=MESH,
-        )
-
-    def pass_on(slot, goal, block):
+            src_ref=stage.at[slot, pl.ds(*part), :], dst_ref=landing.at[pl.ds(*part), :],
+            send_sem=z_send.at[slot], recv_sem=sem,
+            device_id={"tensor": target}, device_id_type=MESH,
+        )
+
+    whole = (0, rows)
+
+    def up_copy(slot, part=whole):
+        return hop_copy(slot, main.at[slot], main_recv.at[slot], z + 1, part)
+
+    def down_copy(slot, part=whole):
+        return hop_copy(slot, main.at[slot], main_recv.at[slot], z - 1, part)
+
+    def last_copy(slot, block, part=whole):
+        return hop_copy(slot, extra.at[block], extra_recv.at[block], z - 1, part)
+
+    def pass_on(slot, goal, block, part=whole):
         @pl.when(goal > z)
         def _():
-            up_copy(slot).start()
+            up_copy(slot, part).start()
 
         @pl.when(goal < z - 1)
         def _():
-            down_copy(slot).start()
+            down_copy(slot, part).start()
 
         @pl.when(goal == z - 1)
         def _():
-            last_copy(slot, block).start()
+            last_copy(slot, block, part).start()
 
     def depth(goal):
         last = n_tensor - 1
         return jnp.where(
             goal > z, z, jnp.where(goal < z, last - z, jnp.maximum(z, last - z))
         )
+
+    def multiply(step, part):
+        owner, piece, late, _ = arrival(step)
+        slot, goal, block = place(owner, piece, late)
+        stage[slot, pl.ds(*part), :] = jnp.dot(
+            gated[late, pl.ds(*part), :],
+            held[owner * PIECES + piece],
+            preferred_element_type=jnp.float32,
+        ).astype(jnp.bfloat16)
+
+        @pl.when(depth(goal) == 0)
+        def _():
+            pass_on(slot, goal, block, part)
+
+    for piece in range(PIECES):
+        send_held(PIECES + piece, PIECES + piece, core_send.at[0], to_core).wait_recv()
+
+    @pl.loop(0, EARLY)
+    def _(step):
+        multiply(step, (FLT, rows - FLT))
+
+    @pl.when(c > 0)
+    def _():
+        halo_copies(c)[1].wait_recv()
+
+    @pl.loop(0, width // LANES)
+    def _(tile):
+        convolve(tile, 0, 1)
+
+    rows_copy = pltpu.make_async_remote_copy(
+        src_ref=gated.at[0], dst_ref=gated.at[1],
+        send_sem=rows_send.at[0], recv_sem=rows_recv.at[0],
+        device_id={"context": to_x}, device_id_type=MESH,
+    )
+    rows_copy.start()
 
     steps = 2 * n_context * PIECES
 
@@ -389,13 +419,13 @@
                 rows_copy.wait_recv()
                 send_away(1).start()
 
-            stage[slot] = jnp.dot(
-                gated[late], held[chunk], preferred_element_type=jnp.float32
-            ).astype(jnp.bfloat16)
-
-            @pl.when(depth(goal) == 0)
-            def _():
-                pass_on(slot, goal, block)
+            @pl.when(step < EARLY)
+            def _():
+                multiply(step, (0, FLT))
+
+            @pl.when(step >= EARLY)
+            def _():
+                multiply(step, whole)
 
         for hop in range(1, n_tensor):
             event = step - hop * LAG
@@ -462,20 +492,22 @@
 
     count = sites.shape[0]
     each = count // n_context
+    folds = SLOTS // each
     row_at = lax.broadcasted_iota(jnp.int32, (n_context * SLOTS, 1), 0)
     local = jnp.full((n_context * SLOTS, 1), -1, jnp.int32)
     for v in range(count):
-        local = jnp.where(
-            row_at == v // each * SLOTS + v % each, sites[v] - c * rows, local
-        )
-    one_hot = (
-        lax.broadcasted_iota(jnp.int32, (n_context * SLOTS, rows), 1) == local
-    ).astype(jnp.float32).astype(jnp.bfloat16)
-    for part in range(width // 256):
-        spot = pl.ds(part * 256, 256)
-        outbox[:, spot] = jnp.dot(
-            one_hot, mixed[:, spot], preferred_element_type=jnp.float32
-        ).astype(jnp.bfloat16)
+        first = v // each * SLOTS
+        mine = jnp.logical_and(row_at // SLOTS * SLOTS == first, row_at % each == v % each)
+        local = jnp.where(mine, sites[v] - c * rows, local)
+    picks = jnp.zeros((n_context * SLOTS, outbox.shape[1]), jnp.float32)
+    for fold in range(folds):
+        here = jnp.where(row_at % SLOTS // each == fold, local, -1)
+        one_hot = (
+            lax.broadcasted_iota(jnp.int32, (n_context * SLOTS, rows), 1) == here
+        ).astype(jnp.float32).astype(jnp.bfloat16)
+        part = pl.ds(fold * outbox.shape[1], outbox.shape[1])
+        picks = picks + jnp.dot(one_hot, mixed[:, part], preferred_element_type=jnp.float32)
+    outbox[...] = picks.astype(jnp.bfloat16)
 
     def pick_copy(step, target):
         return pltpu.make_async_remote_copy(
@@ -492,7 +524,10 @@
     for step, copy in enumerate(picks):
         copy.wait_recv()
         total = total + inbox[step].astype(jnp.float32)
-    picked[...] = total[:each].astype(jnp.bfloat16)
+    for fold in range(folds):
+        picked[:, pl.ds(fold * outbox.shape[1], outbox.shape[1])] = total[
+            fold * each : (fold + 1) * each
+        ].astype(jnp.bfloat16)
 
     for copy in picks:
         copy.wait_send()
@@ -555,8 +590,8 @@
             pltpu.VMEM((2 * chunks, rows, cols), bf),
             pltpu.VMEM((2 * chunks, rows, cols), bf),
             pltpu.VMEM((4 * PIECES, rows, cols), bf),
-            pltpu.VMEM((n_context * SLOTS, 2 * mine), bf),
-            pltpu.VMEM((n_context - 1, SLOTS, 2 * mine), bf),
+            pltpu.VMEM((n_context * SLOTS, 2 * mine * sites // SLOTS), bf),
+            pltpu.VMEM((n_context - 1, SLOTS, 2 * mine * sites // SLOTS), bf),
             dma((2 * PIECES + 1,)),
             dma((2,)),
             dma((2,)),

time: 187 us -> 183 us (0.979)
  Pallas kernels: 182 us -> 178 us
    pallas_call x1, Pallas kernels: 182 us -> 178 us  [fused_on_device(): pl.pallas_call(fused, out_shape=(jax.ShapeDtypeStruct((rows, 2 * mine), b...]
where the time goes in v5:
time: 183 us; the launch traced here: 182 us
  Pallas kernels  178 us (97%)
  local copies, waits for them, and re-layouts  4.06 us (2%)
    pallas_call x1, Pallas kernels, fused_on_device(): pl.pallas_call(fused, out_shape=(jax.ShapeDtypeStruct((rows, 2 * mine), b...  178 us
    unnamed x2, local copies, waits for them, and re-layouts  4.06 us

profile of v5, /device:TPU:0, one launch (start us, length us, event | category | flops | bytes accessed | tf_op | source)
XLA Modules:
  0.0 182.4 jit_solution(10986427231174768002)
XLA Ops:
  0.6 177.7 %shard_map.77 = (bf16[384,2048]{1,0:T(8,128)(2,1)}, bf16[4,2048]{1,0:T(4,128)(2,1)}) custom-call(bf16[3,384,2048]{2,1,0:T(8,128)(2,1)} %proj.1, f32[3,3,2048]{2,1,0:T(4,128)} %taps.1, bf16[128,128]{1,0:T(8,128)(2,1)} %filters.1, f32[1,2048]{1,0:T(1,128)} %bitcast.1, bf16[2048,1024]{1,0:T(8,128)(2,1)} %weight.1, s32[32]{0:T(128)} %sites.1), custom_call_target="tpu_custom_call" | custom-call | flops 12884901888 | bytes 16777216 | tf_op jit(solution)/shard_map/pallas_call | solution.py:573
  178.3 2.7 %copy.10 = bf16[384,2048]{1,0:T(8,128)(2,1)} copy(bf16[384,2048]{1,0:T(8,128)(2,1)} %get-tuple-element.4) | data formatting | bytes 3145728
  181.1 1.3 copy.11

commit v6 on v5

--- a/solution.py
+++ b/solution.py
@@ -98,7 +98,7 @@
 )
 EARLY = 4
 ROWS_STEP = 10
-RELAY_STEP = 18
+RELAY_STEPS = (18, 21)
 
 
 def coded():
@@ -127,7 +127,7 @@
     ext, base, bands, held, away, gated, stage, main, extra, outbox, inbox,
     local_sem, halo_send, halo_recv, x_send, y_send, core_send, held_recv,
     z_send, main_recv, extra_recv, pick_send, pick_recv,
-    rows_send, rows_recv, out_send, out_recv,
+    rows_send, rows_recv, out_send, out_recv, half_send, half_recv, relay_send,
 ):
     _, rows, width = gated.shape
     cols = held.shape[2]
@@ -228,6 +228,25 @@
             device_id={"context": to_x}, device_id_type=MESH,
         )
 
+    swapped = 2 * PIECES + 1
+    deep = held.shape[1] // 2
+
+    def send_half(part):
+        span = pl.ds(part * deep, deep)
+        return pltpu.make_async_remote_copy(
+            src_ref=away.at[1, span, :], dst_ref=held.at[swapped, span, :],
+            send_sem=half_send.at[part], recv_sem=half_recv.at[part],
+            device_id={"context": to_x}, device_id_type=MESH,
+        )
+
+    def relay_half(part):
+        span = pl.ds(part * deep, deep)
+        return pltpu.make_async_remote_copy(
+            src_ref=held.at[swapped, span, :], dst_ref=held.at[6 * PIECES + 1, span, :],
+            send_sem=relay_send.at[part], recv_sem=held_recv.at[6 * PIECES + 1],
+            device_id={"context": to_y}, device_id_type=MESH,
+        )
+
     for piece in range(PIECES):
         away_copies[piece].wait()
         if piece == 0:
@@ -407,17 +426,21 @@
             def _():
                 send_held(chunk, 6 * PIECES + piece, y_send.at[PIECES + piece], to_y).start()
 
-            @pl.when(step == RELAY_STEP)
-            def _():
-                swapped = 2 * PIECES + 1
-                send_away(1).wait_recv()
-                send_held(swapped, 6 * PIECES + 1, y_send.at[PIECES + 1], to_y).start()
-                send_held(swapped, 3 * PIECES + 1, core_send.at[PIECES + 1], to_core).start()
+            for part, when in enumerate(RELAY_STEPS):
+                @pl.when(step == when)
+                def _(part=part):
+                    send_half(part).wait_recv()
+                    relay_half(part).start()
+                    if part == 1:
+                        send_held(
+                            swapped, 3 * PIECES + 1, core_send.at[PIECES + 1], to_core
+                        ).start()
 
             @pl.when(step == ROWS_STEP)
             def _():
                 rows_copy.wait_recv()
-                send_away(1).start()
+                send_half(0).start()
+                send_half(1).start()
 
             @pl.when(step < EARLY)
             def _():
@@ -538,10 +561,13 @@
             copy.wait_send()
 
     rows_copy.wait_send()
-    for piece in range(PIECES):
-        send_away(piece).wait_send()
+    send_away(0).wait_send()
+    for part in (0, 1):
+        send_half(part).wait_send()
+        relay_half(part).wait_send()
     for index in range(2 * PIECES):
-        send_held(0, 0, y_send.at[index], to_y).wait_send()
+        if index < 2 * PIECES - 1:
+            send_held(0, 0, y_send.at[index], to_y).wait_send()
         out_copy(0, index).wait_send()
 
     @pl.loop(0, 4 * PIECES)
@@ -608,6 +634,9 @@
             dma((1,)),
             dma((2 * PIECES,)),
             dma((2 * PIECES,)),
+            dma((2,)),
+            dma((2,)),
+            dma((2,)),
         ],
         compiler_params=pltpu.CompilerParams(
             collective_id=0, has_side_effects=True, vmem_limit_bytes=62 * 1024 * 1024

time: 183 us -> 179 us (0.978)
  Pallas kernels: 178 us -> 174 us
    pallas_call x1, Pallas kernels: 178 us -> 174 us  [fused_on_device(): pl.pallas_call(fused, out_shape=(jax.ShapeDtypeStruct((rows, 2 * mine), b...]
where the time goes in v6:
time: 179 us
  Pallas kernels  174 us (97%)
  local copies, waits for them, and re-layouts  4.06 us (2%)
    pallas_call x1, Pallas kernels, fused_on_device(): pl.pallas_call(fused, out_shape=(jax.ShapeDtypeStruct((rows, 2 * mine), b...  174 us
    unnamed x2, local copies, waits for them, and re-layouts  4.06 us

profile of v6, /device:TPU:0, one launch (start us, length us, event | category | flops | bytes accessed | tf_op | source)
XLA Modules:
  0.0 179.0 jit_solution(14366795581303294575)
XLA Ops:
  0.6 174.3 %shard_map.77 = (bf16[384,2048]{1,0:T(8,128)(2,1)}, bf16[4,2048]{1,0:T(4,128)(2,1)}) custom-call(bf16[3,384,2048]{2,1,0:T(8,128)(2,1)} %proj.1, f32[3,3,2048]{2,1,0:T(4,128)} %taps.1, bf16[128,128]{1,0:T(8,128)(2,1)} %filters.1, f32[1,2048]{1,0:T(1,128)} %bitcast.1, bf16[2048,1024]{1,0:T(8,128)(2,1)} %weight.1, s32[32]{0:T(128)} %sites.1), custom_call_target="tpu_custom_call" | custom-call | flops 12884901888 | bytes 16777216 | tf_op jit(solution)/shard_map/pallas_call | solution.py:599
  175.0 2.7 %copy.10 = bf16[384,2048]{1,0:T(8,128)(2,1)} copy(bf16[384,2048]{1,0:T(8,128)(2,1)} %get-tuple-element.4) | data formatting | bytes 3145728
  177.7 1.3 copy.11
